TPU v7x, 256 devices: a whole 4x4x8 slice. The times are simulated.
256 devices in a mesh: lat: 4 (over y_lo, core), lon: 64 (over x, y_hi, z).
Axes of the slice: x: 4, y: 4 (y_hi: 2, y_lo: 2; y = y_hi * 2 + y_lo), z: 8, core: 2. Of those that a mesh axis runs over, the one named last changes fastest.
Arguments:
- inputs: bfloat16 [48, 1536, 2, 512], P('lat', 'lon'), may hold values from -6 to 6
- shift_lat: int32 [1], replicated, may hold values from 1 to 5
- shift_lon: int32 [1], replicated, may hold values from 1 to 11
- gain_attn: float32 [512], replicated, may hold values from 0.1 to 1.9
- w_qkv: bfloat16 [512, 1536], replicated, may hold values from -0.25 to 0.25
- w_out: bfloat16 [512, 512], replicated, may hold values from -0.25 to 0.25
- gain_merge: float32 [2048], replicated, may hold values from 0.1 to 1.9
- w_merge: bfloat16 [2048, 1024], replicated, may hold values from -0.125 to 0.125
- cot_coarse: bfloat16 [24, 768, 2, 1024], P('lat', 'lon'), may hold values from -6 to 6
- cot_skip: bfloat16 [48, 1536, 2, 512], P('lat', 'lon'), may hold values from -6 to 6
Outputs:
- coarse: bfloat16 [24, 768, 2, 1024], P('lat', 'lon')
- skip: bfloat16 [48, 1536, 2, 512], P('lat', 'lon')
- grad_input: bfloat16 [48, 1536, 2, 512], P('lat', 'lon')
All inputs are finite; a program needn't handle non-finite values.
Results may differ from a plain program's by a relative error of at most 0.015.
Values may be sent and summed in bfloat16 or wider, within the bound.
A program may use at most 128 MiB of HBM per device.

v0:
```python
import jax
import jax.numpy as jnp
from jax import lax
from jax.sharding import PartitionSpec as P

HEADS = 8
WLAT = 6
WLON = 12


def from_behind(value, axis, steps):
    count = lax.axis_size(axis)
    pairs = [(source, (source + steps) % count) for source in range(count)]
    return lax.ppermute(value, axis, pairs)


def normalize(values_in):
    row_mean = jnp.mean(values_in, -1, keepdims=True)
    centred = values_in - row_mean
    variance = jnp.mean(centred * centred, -1, keepdims=True)
    return centred * lax.rsqrt(variance + 1e-05)


def to_windows(field):
    lat_rows, lon_cols, level_count, feature_width = field.shape
    shaped = field.reshape(
        lat_rows // WLAT, WLAT, lon_cols // WLON, WLON, level_count, feature_width
    )
    return shaped.transpose(0, 2, 1, 3, 4, 5).reshape(-1, WLAT * WLON * level_count, feature_width)


def from_windows(field, lat_rows, lon_cols, level_count):
    feature_width = field.shape[-1]
    shaped = field.reshape(
        lat_rows // WLAT, lon_cols // WLON, WLAT, WLON, level_count, feature_width
    )
    return shaped.transpose(0, 2, 1, 3, 4, 5).reshape(
        lat_rows, lon_cols, level_count, feature_width
    )


def attend(windows, regions, head_count):
    window_count, token_count, triple_width = windows.shape
    feature_width = triple_width // 3
    head_size = feature_width // head_count
    query_part = windows[..., :feature_width].reshape(
        window_count, token_count, head_count, head_size
    )
    key_part = windows[..., feature_width : 2 * feature_width].reshape(
        window_count, token_count, head_count, head_size
    )
    value_part = windows[..., 2 * feature_width :].reshape(
        window_count, token_count, head_count, head_size
    )
    scores = jnp.einsum(
        "wthd,wshd->whts", query_part, key_part, preferred_element_type=jnp.float32
    ) * head_size ** (-0.5)
    same_region = regions[:, None, :, None] == regions[:, None, None, :]
    scores = jnp.where(same_region, scores, jnp.float32(-1e30))
    row_top = lax.stop_gradient(jnp.max(scores, -1, keepdims=True))
    exp_scores = jnp.exp(scores - row_top)
    soft_weights = (exp_scores / jnp.sum(exp_scores, -1, keepdims=True)).astype(jnp.bfloat16)
    mixed = jnp.einsum(
        "whts,wshd->wthd", soft_weights, value_part, preferred_element_type=jnp.float32
    )
    return mixed.astype(jnp.bfloat16).reshape(window_count, token_count, feature_width)


def attention_branch(rolled, region_rows, gain_attn, w_qkv, w_out):
    lat_rows, lon_cols, level_count, feature_width = rolled.shape
    normed_tokens = (normalize(rolled.astype(jnp.float32)) * gain_attn).astype(jnp.bfloat16)
    projected = jnp.dot(normed_tokens, w_qkv, preferred_element_type=jnp.float32).astype(
        jnp.bfloat16
    )
    windows = to_windows(projected)
    region_field = jnp.broadcast_to(
        region_rows[:, None, None, None], (lat_rows, lon_cols, level_count, 1)
    )
    regions = to_windows(region_field)[..., 0]
    mixed = attend(windows, regions, HEADS)
    unwindowed = from_windows(mixed, lat_rows, lon_cols, level_count)
    return jnp.dot(unwindowed, w_out, preferred_element_type=jnp.float32).astype(jnp.bfloat16)


def merge_patches(skip, gain_merge, w_merge):
    lat_rows, lon_cols, level_count, feature_width = skip.shape
    grouped = skip.reshape(lat_rows // 2, 2, lon_cols // 2, 2, level_count, feature_width)
    grouped = grouped.transpose(0, 2, 4, 1, 3, 5).reshape(
        lat_rows // 2, lon_cols // 2, level_count, 4 * feature_width
    )
    merged = (normalize(grouped.astype(jnp.float32)) * gain_merge).astype(jnp.bfloat16)
    return jnp.dot(merged, w_merge, preferred_element_type=jnp.float32).astype(jnp.bfloat16)


def extend_ahead(block):
    rows_next = from_behind(block[:WLAT], "lat", -1)
    widened = jnp.concatenate([block, rows_next], 0)
    columns_next = from_behind(widened[:, :WLON], "lon", -1)
    return jnp.concatenate([widened, columns_next], 1)


def extend_behind(block):
    rows_prior = from_behind(block[-WLAT:], "lat", 1)
    widened = jnp.concatenate([rows_prior, block], 0)
    columns_prior = from_behind(widened[:, -WLON:], "lon", 1)
    return jnp.concatenate([columns_prior, widened], 1)


def local(
    inputs, shift_lat, shift_lon, gain_attn, w_qkv, w_out, gain_merge, w_merge, cot_coarse, cot_skip
):
    lat_rows, lon_cols, level_count, feature_width = inputs.shape
    lat_shift = shift_lat[0]
    lon_shift = shift_lon[0]
    index_zero = jnp.zeros((), jnp.int32)
    tile_shape = (lat_rows, lon_cols, level_count, feature_width)
    ahead_start = (lat_shift, lon_shift, index_zero, index_zero)
    behind_start = (WLAT - lat_shift, WLON - lon_shift, index_zero, index_zero)
    band_rows = lat_rows * lax.axis_size("lat")
    lat_pos = lax.axis_index("lat") * lat_rows + jnp.arange(lat_rows, dtype=jnp.int32)
    region_rows = (lat_pos >= band_rows - lat_shift).astype(jnp.int32)

    def branch_fn(field):
        return attention_branch(field, region_rows, gain_attn, w_qkv, w_out)

    def merge_fn(field):
        return merge_patches(field, gain_merge, w_merge)

    rolled = lax.dynamic_slice(extend_ahead(inputs), ahead_start, tile_shape)
    branch, branch_back = jax.vjp(branch_fn, rolled)
    placed = lax.dynamic_slice(extend_behind(branch), behind_start, tile_shape)
    skip = (inputs.astype(jnp.float32) + placed.astype(jnp.float32)).astype(jnp.bfloat16)
    coarse, merge_back = jax.vjp(merge_fn, skip)
    grad_skip = merge_back(cot_coarse)[0] + cot_skip
    grad_branch = lax.dynamic_slice(extend_ahead(grad_skip), ahead_start, tile_shape)
    grad_rolled = branch_back(grad_branch)[0]
    grad_input = grad_skip + lax.dynamic_slice(extend_behind(grad_rolled), behind_start, tile_shape)
    return (coarse, skip, grad_input)


def solution(mesh):
    placed = (
        P("lat", "lon", None, None),
        P(),
        P(),
        P(),
        P(),
        P(),
        P(),
        P(),
        P("lat", "lon", None, None),
        P("lat", "lon", None, None),
    )
    return jax.shard_map(
        local,
        mesh=mesh,
        in_specs=placed,
        out_specs=(
            P("lat", "lon", None, None),
            P("lat", "lon", None, None),
            P("lat", "lon", None, None),
        ),
        check_vma=False,
    )
```

profile of v0, /device:TPU:0, one launch (start us, length us, event | category | flops | bytes accessed | tf_op | source)
XLA Modules:
  0.0 209.3 jit_solution(14249683265195409498)
XLA Ops:
  2.2 4.1 %collective-permute-done = bf16[6,24,2,512]{3,1,2,0:T(8,128)(2,1)S(1)} collective-permute-done((bf16[6,24,2,512]{3,1,2,0:T(8,128)(2,1)S(1)}, bf16[6,24,2,512]{3,1,2,0:T(8,128)(2,1)S(1)}, u32[]{:S(2)}, u32[]{:S(2)}) %collective-permute-start) | collective-permute-done | bytes 294944 | tf_op jit(solution)/shard_map/ppermute | solution.py:14
  6.9 10.3 %collective-permute-start.1 = (bf16[18,12,2,512]{3,2,1,0:T(2,128)(2,1)S(1)}, bf16[18,12,2,512]{3,2,1,0:T(2,128)(2,1)}, u32[]{:S(2)}, u32[]{:S(2)}) collective-permute-start(bf16[18,12,2,512]{3,2,1,0:T(2,128)(2,1)S(1)} %copy.159), channel_id=1, source_target_pairs={{0,63},{1,0},{2,1},{3,2},{4,3},{5,4},{6,5},{7,6},{8,7},{9,8},{10,9... | collective-permute-start | bytes 1327112 | tf_op jit(solution)/shard_map/ppermute | solution.py:14
  18.9 8.8 %collective-permute-done.1 = bf16[18,12,2,512]{3,2,1,0:T(2,128)(2,1)} collective-permute-done((bf16[18,12,2,512]{3,2,1,0:T(2,128)(2,1)S(1)}, bf16[18,12,2,512]{3,2,1,0:T(2,128)(2,1)}, u32[]{:S(2)}, u32[]{:S(2)}) %collective-permute-start.1) | collective-permute-done | bytes 442400 | tf_op jit(solution)/shard_map/ppermute | solution.py:14
  32.6 2.5 %copy.162 = bf16[2,2,6,12,2,1536]{5,4,3,2,1,0:T(2,128)(2,1)} copy(bf16[2,2,6,12,2,1536]{5,4,3,1,2,0:T(2,128)(2,1)S(1)} %bitcast.112) | data formatting | bytes 3538944 | tf_op jit(solution)/shard_map/jvp()/transpose | solution.py:29
  35.1 4.8 %reshape.147 = bf16[4,144,1536]{2,1,0:T(8,128)(2,1)} reshape(bf16[2,2,6,12,2,1536]{5,4,3,2,1,0:T(2,128)(2,1)} %copy.162) | data formatting | bytes 3538944 | tf_op jit(solution)/shard_map/jvp()/reshape | solution.py:29
  39.9 2.4 %fusion.96 = (bf16[4,144,512]{2,1,0:T(8,128)(2,1)S(1)}, bf16[4,144,512]{2,1,0:T(8,128)(2,1)S(1)}, bf16[4,144,512]{2,1,0:T(8,128)(2,1)}) fusion(bf16[4,144,1536]{2,1,0:T(8,128)(2,1)} %reshape.147), kind=kLoop, calls=%fused_computation.121 | loop fusion | bytes 3538944 | tf_op jit(solution)/shard_map/jvp()/slice | solution.py:49
  46.3 5.9 %fusion.97 = (f32[4,8,144]{2,1,0:T(8,128)S(1)}, f32[4,8,144,144]{2,3,1,0:T(8,128)}) fusion(pred[4,144,144]{1,2,0:T(8,128)(4,1)S(1)} %broadcast_compare_fusion, bf16[4,144,8,64]{1,3,2,0:T(8,128)(2,1)} %bitcast.121, bf16[4,144,8,64]{1,3,2,0:T(8,128)(2,1)} %bitcast.123), kind=kOutput, calls=%fused_computation.122 | convolution fusion | flops 87589008 | bytes 3935232 | tf_op jit(solution)/shard_map/jvp()/sub | solution.py:61
  52.3 2.8 %divide_convert_fusion = bf16[4,8,144,144]{2,3,1,0:T(8,128)(2,1)S(1)} fusion(f32[4,8,144,144]{2,3,1,0:T(8,128)} %get-tuple-element.26, f32[4,8,144]{2,1,0:T(8,128)S(1)} %get-tuple-element.25), kind=kLoop, calls=%fused_computation.9 | loop fusion | flops 1327104 | bytes 3999744 | tf_op jit(solution)/shard_map/jvp()/convert_element_type | solution.py:62
  64.8 5.9 %collective-permute-done.2 = bf16[6,24,2,512]{3,1,2,0:T(8,128)(2,1)S(1)} collective-permute-done((bf16[6,24,2,512]{3,1,2,0:T(8,128)(2,1)S(1)}, bf16[6,24,2,512]{3,1,2,0:T(8,128)(2,1)S(1)}, u32[]{:S(2)}, u32[]{:S(2)}) %collective-permute-start.2) | collective-permute-done | bytes 294944 | tf_op jit(solution)/shard_map/ppermute | solution.py:14
  72.9 16.9 %collective-permute-done.3 = bf16[18,12,2,512]{3,2,1,0:T(2,128)(2,1)} collective-permute-done((bf16[18,12,2,512]{3,2,1,0:T(2,128)(2,1)}, bf16[18,12,2,512]{3,2,1,0:T(2,128)(2,1)}, u32[]{:S(2)}, u32[]{:S(2)}) %collective-permute-start.3) | collective-permute-done | bytes 442400 | tf_op jit(solution)/shard_map/ppermute | solution.py:14
  90.8 2.3 %add_convert_fusion.2 = bf16[12,24,2,512]{3,1,2,0:T(8,128)(2,1)} fusion(s32[]{:T(128)S(6)} %select_n.27, s32[]{:T(128)S(6)} %select_n.28, bf16[18,12,2,512]{3,1,2,0:T(8,128)(2,1)S(1)} %copy.171, bf16[6,24,2,512]{3,1,2,0:T(8,128)(2,1)} %copy-done.8, bf16[12,24,2,512]{3,1,2,0:T(8,128)(2,1)S(1)} %convolution_convert_fusion.7, ...), kind=kLoop, calls=%fused_computation.75 | loop fusion | flops 2654208 | bytes 2506760 | tf_op jit(solution)/shard_map/convert_element_type | solution.py:132
  98.4 2.7 %reshape.162 = f32[6,12,2,2048]{3,2,1,0:T(2,128)S(1)} reshape(f32[6,12,2,2,2,512]{5,4,3,2,1,0:T(2,128)} %bitcast.114) | data formatting | bytes 2359296 | tf_op jit(solution)/shard_map/jvp()/convert_element_type | solution.py:91
  101.1 4.4 %fusion.33 = (f32[6,12,2]{1,2,0:T(2,128)S(1)}, f32[6,12,2,2048]{3,1,2,0:T(8,128)S(1)}) fusion(f32[6,12,2,2048]{3,2,1,0:T(2,128)S(1)} %reshape.162, f32[6,12,2]{1,2,0:T(2,128)S(1)} %broadcast_multiply_fusion.1, f32[2048]{0:T(1024)S(1)} %copy-done.17, bf16[2048,1024]{1,0:T(8,128)(2,1)} %param.17, bf16[6,12,2,1024]{3,2,1,0:T(2,128)(2,1)} %param.18), kind=kOutput, calls=%fused_computation.38 | convolution fusion | flops 605749120 | bytes 6857856 | tf_op jit(solution)/shard_map/transpose(jvp())/dot_general | solution.py:92
  108.1 2.9 %reshape.168 = bf16[6,12,2,2,2,512]{5,4,3,1,2,0:T(2,128)(2,1)} reshape(bf16[6,12,2,2048]{3,1,2,0:T(8,128)(2,1)} %add_convert_fusion) | data formatting | bytes 1179648 | tf_op jit(solution)/shard_map/transpose(jvp())/reshape | solution.py:88
  111.0 2.4 %copy.179 = bf16[6,2,12,2,2,512]{5,3,2,4,1,0:T(2,128)(2,1)} copy(bf16[6,2,12,2,2,512]{5,3,1,2,4,0:T(2,128)(2,1)} %bitcast.119) | data formatting | bytes 1179648 | tf_op jit(solution)/shard_map/transpose(jvp())/transpose | solution.py:88
  113.4 2.6 %reshape.154 = bf16[12,24,2,512]{3,1,2,0:T(8,128)(2,1)} reshape(bf16[6,2,12,2,2,512]{5,3,2,4,1,0:T(2,128)(2,1)} %copy.179) | data formatting | bytes 1179648 | tf_op jit(solution)/shard_map/transpose(jvp())/reshape | solution.py:87
  117.7 4.2 %collective-permute-done.4 = bf16[6,24,2,512]{3,1,2,0:T(8,128)(2,1)S(1)} collective-permute-done((bf16[6,24,2,512]{3,1,2,0:T(8,128)(2,1)S(1)}, bf16[6,24,2,512]{3,1,2,0:T(8,128)(2,1)S(1)}, u32[]{:S(2)}, u32[]{:S(2)}) %collective-permute-start.4) | collective-permute-done | bytes 294944 | tf_op jit(solution)/shard_map/ppermute | solution.py:14
  124.3 10.9 %collective-permute-done.5 = bf16[18,12,2,512]{3,2,1,0:T(2,128)(2,1)S(1)} collective-permute-done((bf16[18,12,2,512]{3,2,1,0:T(2,128)(2,1)S(1)}, bf16[18,12,2,512]{3,2,1,0:T(2,128)(2,1)S(1)}, u32[]{:S(2)}, u32[]{:S(2)}) %collective-permute-start.5) | collective-permute-done | bytes 442400 | tf_op jit(solution)/shard_map/ppermute | solution.py:14
  138.1 3.2 %reshape.156 = bf16[4,144,8,64]{3,2,1,0:T(8,128)(2,1)} reshape(bf16[2,2,6,12,2,512]{5,4,3,2,1,0:T(2,128)(2,1)} %copy.184) | data formatting | bytes 1179648 | tf_op jit(solution)/shard_map/transpose(jvp())/reshape;transpose(jvp())/reshape | solution.py:66
  141.3 2.6 %copy.185 = bf16[4,8,64,144]{3,2,1,0:T(8,128)(2,1)} copy(bf16[4,8,64,144]{2,1,3,0:T(8,128)(2,1)} %bitcast.115) | data formatting | bytes 1179648 | tf_op jit(solution)/shard_map/transpose(jvp(whts,wshd->wthd))/transpose | solution.py:63
  143.9 4.0 %convolution_convert_fusion.4 = bf16[4,8,64,144]{3,2,1,0:T(8,128)(2,1)} fusion(bf16[4,8,64,144]{3,2,1,0:T(8,128)(2,1)} %copy.185, bf16[4,8,144,144]{2,3,1,0:T(8,128)(2,1)} %copy-done.1), kind=kOutput, calls=%fused_computation.42 | convolution fusion | flops 85229568 | bytes 2506752 | tf_op jit(solution)/shard_map/transpose(jvp(whts,wshd->wthd))/dot_general | solution.py:63
  147.9 4.2 %fusion.6 = (f32[4,8,144]{2,1,0:T(8,128)S(1)}, bf16[4,8,144,144]{2,3,1,0:T(8,128)(2,1)S(1)}) fusion(f32[4,8,144,144]{2,3,1,0:T(8,128)} %get-tuple-element.26, f32[4,8,144]{2,1,0:T(8,128)S(1)} %multiply_divide_fusion, bf16[4,8,64,144]{3,2,1,0:T(8,128)(2,1)} %copy.185, bf16[4,144,8,64]{1,3,2,0:T(8,128)(2,1)} %bitcast.111), kind=kOutput, calls=%fused_computation.8 | convolution fusion | flops 88247808 | bytes 5197824 | tf_op jit(solution)/shard_map/transpose(jvp(whts,wshd->wthd))/dot_general | solution.py:63
  152.1 2.4 %convolution_convert_fusion.2 = bf16[4,8,144,64]{2,3,1,0:T(8,128)(2,1)} fusion(bf16[4,144,8,64]{1,3,2,0:T(8,128)(2,1)S(1)} %bitcast.124, f32[4,8,144,144]{2,3,1,0:T(8,128)S(1)} %bitcast.109, bf16[4,8,144,144]{2,3,1,0:T(8,128)(2,1)S(1)} %get-tuple-element.30, f32[4,8,144]{2,1,0:T(8,128)S(1)} %neg.13, f32[4,8,144]{2,1,0:T(8,128)S(1)} %get-tuple-element.25, ...), kind=kOutput, calls=%fused_computation.40 | convolution fusion | flops 89210880 | bytes 5280768 | tf_op jit(solution)/shard_map/transpose(jvp(wthd,wshd->whts))/dot_general | solution.py:55
  154.5 2.6 %convolution_convert_fusion.3 = bf16[4,8,144,64]{2,3,1,0:T(8,128)(2,1)} fusion(bf16[4,144,8,64]{1,3,2,0:T(8,128)(2,1)S(1)} %bitcast.122, f32[4,8,144,144]{2,3,1,0:T(8,128)S(1)} %bitcast.109, bf16[4,8,144,144]{2,3,1,0:T(8,128)(2,1)S(1)} %get-tuple-element.30, f32[4,8,144]{2,1,0:T(8,128)S(1)} %neg.13, f32[4,8,144]{2,1,0:T(8,128)S(1)} %get-tuple-element.25, ...), kind=kOutput, calls=%fused_computation.41 | convolution fusion | flops 89210880 | bytes 5280768 | tf_op jit(solution)/shard_map/transpose(jvp(wthd,wshd->whts))/dot_general | solution.py:55
  157.1 2.2 %copy.187 = bf16[4,144,512]{2,1,0:T(8,128)(2,1)} copy(bf16[4,144,512]{1,2,0:T(8,128)(2,1)} %bitcast.116) | data formatting | bytes 1179648 | tf_op jit(solution)/shard_map/transpose(jvp())/reshape | solution.py:52
  159.3 2.2 %copy.190 = bf16[4,144,512]{2,1,0:T(8,128)(2,1)} copy(bf16[4,144,512]{1,2,0:T(8,128)(2,1)} %bitcast.126) | data formatting | bytes 1179648 | tf_op jit(solution)/shard_map/transpose(jvp())/reshape | solution.py:49
  161.4 2.1 %copy.192 = bf16[4,144,512]{2,1,0:T(8,128)(2,1)} copy(bf16[4,144,512]{1,2,0:T(8,128)(2,1)} %bitcast.125) | data formatting | bytes 1179648 | tf_op jit(solution)/shard_map/transpose(jvp())/reshape | solution.py:46
  163.6 2.8 %pad_add_fusion = bf16[4,144,1536]{2,1,0:T(8,128)(2,1)} fusion(bf16[4,144,512]{2,1,0:T(8,128)(2,1)} %copy.192, bf16[4,144,512]{2,1,0:T(8,128)(2,1)} %copy.190, bf16[4,144,512]{2,1,0:T(8,128)(2,1)} %copy.187), kind=kLoop, calls=%fused_computation.28 | loop fusion | flops 5308416 | bytes 3538944 | tf_op jit(solution)/shard_map/transpose(jvp())/add_any | solution.py:46
  166.3 4.7 %reshape.160 = bf16[2,2,6,12,2,1536]{5,4,3,2,1,0:T(2,128)(2,1)} reshape(bf16[4,144,1536]{2,1,0:T(8,128)(2,1)} %pad_add_fusion) | data formatting | bytes 3538944 | tf_op jit(solution)/shard_map/transpose(jvp())/reshape | solution.py:29
  171.0 3.0 %copy.193 = bf16[2,6,2,12,2,1536]{5,4,3,2,1,0:T(2,128)(2,1)S(1)} copy(bf16[2,6,2,12,2,1536]{5,4,3,1,2,0:T(2,128)(2,1)} %bitcast.113) | data formatting | bytes 3538944 | tf_op jit(solution)/shard_map/transpose(jvp())/transpose | solution.py:29
  176.8 15.4 %collective-permute-done.6 = bf16[6,24,2,512]{3,1,2,0:T(8,128)(2,1)S(1)} collective-permute-done((bf16[6,24,2,512]{3,1,2,0:T(8,128)(2,1)S(1)}, bf16[6,24,2,512]{3,1,2,0:T(8,128)(2,1)S(1)}, u32[]{:S(2)}, u32[]{:S(2)}) %collective-permute-start.6) | collective-permute-done | bytes 294944 | tf_op jit(solution)/shard_map/ppermute | solution.py:14
  196.9 10.1 %collective-permute-done.7 = bf16[18,12,2,512]{3,2,1,0:T(2,128)(2,1)S(1)} collective-permute-done((bf16[18,12,2,512]{3,2,1,0:T(2,128)(2,1)S(1)}, bf16[18,12,2,512]{3,2,1,0:T(2,128)(2,1)S(1)}, u32[]{:S(2)}, u32[]{:S(2)}) %collective-permute-start.7) | collective-permute-done | bytes 442400 | tf_op jit(solution)/shard_map/ppermute | solution.py:14
  (115 shorter events, 48.4 us)
Async XLA Ops:
  0.6 29.1 %copy-start = (bf16[512,1536]{1,0:T(8,128)(2,1)S(1)}, bf16[512,1536]{1,0:T(8,128)(2,1)}, u32[]{:S(2)}) copy-start(bf16[512,1536]{1,0:T(8,128)(2,1)} %param.14) | copy-start | bytes 4718596
  0.6 1.5 copy-start.6
  2.0 4.3 %collective-permute-start = (bf16[6,24,2,512]{3,1,2,0:T(8,128)(2,1)S(1)}, bf16[6,24,2,512]{3,1,2,0:T(8,128)(2,1)S(1)}, u32[]{:S(2)}, u32[]{:S(2)}) collective-permute-start(bf16[6,24,2,512]{3,1,2,0:T(8,128)(2,1)S(1)} %copy.249), channel_id=1, source_target_pairs={{0,192},{64,0},{128,64},{192,128},{1,193},{65,1},{129,65},{193,129... | collective-permute-start | bytes 884744 | tf_op jit(solution)/shard_map/ppermute | solution.py:14
  6.9 20.8 %collective-permute-start.1 = (bf16[18,12,2,512]{3,2,1,0:T(2,128)(2,1)S(1)}, bf16[18,12,2,512]{3,2,1,0:T(2,128)(2,1)}, u32[]{:S(2)}, u32[]{:S(2)}) collective-permute-start(bf16[18,12,2,512]{3,2,1,0:T(2,128)(2,1)S(1)} %copy.159), channel_id=1, source_target_pairs={{0,63},{1,0},{2,1},{3,2},{4,3},{5,4},{6,5},{7,6},{8,7},{9,8},{10,9... | collective-permute-start | bytes 1327112 | tf_op jit(solution)/shard_map/ppermute | solution.py:14
  18.9 27.4 %copy-start.11 = (pred[4,144,144]{1,2,0:T(8,128)(4,1)}, pred[4,144,144]{1,2,0:T(8,128)(4,1)S(1)}, u32[]{:S(2)}) copy-start(pred[4,144,144]{1,2,0:T(8,128)(4,1)S(1)} %broadcast_compare_fusion) | copy-start | bytes 248836
  28.8 1.0 copy-start.18
  29.7 1.2 copy-start.13
  46.3 8.8 %copy-start.2 = (bf16[4,144,512]{1,2,0:T(8,128)(2,1)}, bf16[4,144,512]{1,2,0:T(8,128)(2,1)S(1)}, u32[]{:S(2)}) copy-start(bf16[4,144,512]{1,2,0:T(8,128)(2,1)S(1)} %copy.163) | copy-start | bytes 1769476
  55.1 1.4 copy-start.1
  64.3 26.5 %copy-start.7 = (bf16[12,24,2,512]{3,2,1,0:T(2,128)(2,1)S(1)}, bf16[12,24,2,512]{3,2,1,0:T(2,128)(2,1)}, u32[]{:S(2)}) copy-start(bf16[12,24,2,512]{3,2,1,0:T(2,128)(2,1)} %param.10) | copy-start | bytes 1769476
  64.4 6.4 %collective-permute-start.2 = (bf16[6,24,2,512]{3,1,2,0:T(8,128)(2,1)S(1)}, bf16[6,24,2,512]{3,1,2,0:T(8,128)(2,1)S(1)}, u32[]{:S(2)}, u32[]{:S(2)}) collective-permute-start(bf16[6,24,2,512]{3,1,2,0:T(8,128)(2,1)S(1)} %slice.49), channel_id=1, source_target_pairs={{0,64},{64,128},{128,192},{192,0},{1,65},{65,129},{129,193},{193,1... | collective-permute-start | bytes 884744 | tf_op jit(solution)/shard_map/ppermute | solution.py:14
  70.8 0.7 copy-start.8
  72.9 16.9 %collective-permute-start.3 = (bf16[18,12,2,512]{3,2,1,0:T(2,128)(2,1)}, bf16[18,12,2,512]{3,2,1,0:T(2,128)(2,1)}, u32[]{:S(2)}, u32[]{:S(2)}) collective-permute-start(bf16[18,12,2,512]{3,2,1,0:T(2,128)(2,1)} %copy.170), channel_id=1, source_target_pairs={{0,1},{1,2},{2,3},{3,4},{4,5},{5,6},{6,7},{7,8},{8,9},{9,10},{10,1... | collective-permute-start | bytes 1327112 | tf_op jit(solution)/shard_map/ppermute | solution.py:14
  97.4 3.7 %copy-start.17 = (f32[2048]{0:T(1024)S(1)}, f32[2048]{0:T(1024)}, u32[]{:S(2)}) copy-start(f32[2048]{0:T(1024)} %param.16) | copy-start | bytes 24580
  117.4 18.0 %copy-start.3 = (bf16[12,24,2,512]{3,1,2,0:T(8,128)(2,1)}, bf16[12,24,2,512]{3,1,2,0:T(8,128)(2,1)S(1)}, u32[]{:S(2)}) copy-start(bf16[12,24,2,512]{3,1,2,0:T(8,128)(2,1)S(1)} %copy_add_fusion) | copy-start | bytes 1769476
  117.4 17.9 %copy-start.16 = (bf16[512,512]{1,0:T(8,128)(2,1)S(1)}, bf16[512,512]{1,0:T(8,128)(2,1)}, u32[]{:S(2)}) copy-start(bf16[512,512]{1,0:T(8,128)(2,1)} %param.15) | copy-start | bytes 1572868
  117.4 4.5 %collective-permute-start.4 = (bf16[6,24,2,512]{3,1,2,0:T(8,128)(2,1)S(1)}, bf16[6,24,2,512]{3,1,2,0:T(8,128)(2,1)S(1)}, u32[]{:S(2)}, u32[]{:S(2)}) collective-permute-start(bf16[6,24,2,512]{3,1,2,0:T(8,128)(2,1)S(1)} %slice.50), channel_id=1, source_target_pairs={{0,192},{64,0},{128,64},{192,128},{1,193},{65,1},{129,65},{193,129... | collective-permute-start | bytes 884744 | tf_op jit(solution)/shard_map/ppermute | solution.py:14
  122.5 12.7 %collective-permute-start.5 = (bf16[18,12,2,512]{3,2,1,0:T(2,128)(2,1)S(1)}, bf16[18,12,2,512]{3,2,1,0:T(2,128)(2,1)S(1)}, u32[]{:S(2)}, u32[]{:S(2)}) collective-permute-start(bf16[18,12,2,512]{3,2,1,0:T(2,128)(2,1)S(1)} %copy.181), channel_id=1, source_target_pairs={{0,63},{1,0},{2,1},{3,2},{4,3},{5,4},{6,5},{7,6},{8,7},{9,8},{10,9... | collective-permute-start | bytes 1327112 | tf_op jit(solution)/shard_map/ppermute | solution.py:14
  143.9 8.2 %slice-start = ((s8[4718592]{0:T(1024)(128)(4,1)}), s8[4194304]{0:T(1024)(128)(4,1)S(1)}, s32[]{:S(2)}) async-start(s8[4718592]{0:T(1024)(128)(4,1)} %bitcast.108), calls=%async_computation | async-start | bytes 8388608
  147.9 4.2 %slice-start.1 = ((s8[4718592]{0:T(1024)(128)(4,1)}), s8[524288]{0:T(1024)(128)(4,1)S(1)}, s32[]{:S(2)}) async-start(s8[4718592]{0:T(1024)(128)(4,1)} %bitcast.108), calls=%async_computation.1 | async-start | bytes 1048576
  147.9 4.2 %copy-start.10 = (bf16[4,144,512]{1,2,0:T(8,128)(2,1)S(1)}, bf16[4,144,512]{1,2,0:T(8,128)(2,1)}, u32[]{:S(2)}) copy-start(bf16[4,144,512]{1,2,0:T(8,128)(2,1)} %copy.165) | copy-start | bytes 1769476
  147.9 4.2 %copy-start.12 = (pred[4,144,144]{1,2,0:T(8,128)(4,1)S(1)}, pred[4,144,144]{1,2,0:T(8,128)(4,1)}, u32[]{:S(2)}) copy-start(pred[4,144,144]{1,2,0:T(8,128)(4,1)} %copy-done.11) | copy-start | bytes 248836
  152.1 2.4 %copy-start.9 = (bf16[4,144,512]{1,2,0:T(8,128)(2,1)S(1)}, bf16[4,144,512]{1,2,0:T(8,128)(2,1)}, u32[]{:S(2)}) copy-start(bf16[4,144,512]{1,2,0:T(8,128)(2,1)} %copy.164) | copy-start | bytes 1769476
  174.0 1.2 copy-start.14
  175.8 18.4 %copy-start.15 = (bf16[2048,1024]{1,0:T(8,128)(2,1)S(1)}, bf16[2048,1024]{1,0:T(8,128)(2,1)}, u32[]{:S(2)}) copy-start(bf16[2048,1024]{1,0:T(8,128)(2,1)} %param.17) | copy-start | bytes 12582916
  176.2 16.7 %copy-start.5 = (bf16[12,24,2,512]{3,1,2,0:T(8,128)(2,1)S(1)}, bf16[12,24,2,512]{3,1,2,0:T(8,128)(2,1)}, u32[]{:S(2)}) copy-start(bf16[12,24,2,512]{3,1,2,0:T(8,128)(2,1)} %add_convert_fusion.2) | copy-start | bytes 1769476
  176.2 16.0 %collective-permute-start.6 = (bf16[6,24,2,512]{3,1,2,0:T(8,128)(2,1)S(1)}, bf16[6,24,2,512]{3,1,2,0:T(8,128)(2,1)S(1)}, u32[]{:S(2)}, u32[]{:S(2)}) collective-permute-start(bf16[6,24,2,512]{3,1,2,0:T(8,128)(2,1)S(1)} %slice.51), channel_id=1, source_target_pairs={{0,64},{64,128},{128,192},{192,0},{1,65},{65,129},{129,193},{193,1... | collective-permute-start | bytes 884744 | tf_op jit(solution)/shard_map/ppermute | solution.py:14
  192.8 14.1 %collective-permute-start.7 = (bf16[18,12,2,512]{3,2,1,0:T(2,128)(2,1)S(1)}, bf16[18,12,2,512]{3,2,1,0:T(2,128)(2,1)S(1)}, u32[]{:S(2)}, u32[]{:S(2)}) collective-permute-start(bf16[18,12,2,512]{3,2,1,0:T(2,128)(2,1)S(1)} %copy.195), channel_id=1, source_target_pairs={{0,1},{1,2},{2,3},{3,4},{4,5},{5,6},{6,7},{7,8},{8,9},{9,10},{10,1... | collective-permute-start | bytes 1327112 | tf_op jit(solution)/shard_map/ppermute | solution.py:14
  195.8 11.2 %copy-start.4 = (bf16[12,24,2,512]{3,1,2,0:T(8,128)(2,1)S(1)}, bf16[12,24,2,512]{3,1,2,0:T(8,128)(2,1)}, u32[]{:S(2)}) copy-start(bf16[12,24,2,512]{3,1,2,0:T(8,128)(2,1)} %copy-done.3) | copy-start | bytes 1769476
where the time goes:
time: 213 us; the launch traced here: 209 us
  waiting for transfers between devices  76.3 us (36%)
  local copies, waits for them, and re-layouts  68.9 us (32%)
  matrix products  31.4 us (15%)
  other arithmetic  16.3 us (8%)
  starting transfers between devices  13.6 us (6%)
  between operations  2.85 us (1%)
    ppermute x8, waiting for transfers between devices, from_behind(): return lax.ppermute(value, axis, pairs)  76.3 us
    ppermute x8, starting transfers between devices, from_behind(): return lax.ppermute(value, axis, pairs)  13.6 us
    dot_general x3, matrix products, attend(): jnp.einsum('whts,wshd->wthd', soft_weights, value_part, preferred_element...  9.63 us
    reshape x2, local copies, waits for them, and re-layouts, to_windows(): shaped.transpose(0, 2, 1, 3, 4, 5)  9.49 us
    convert_element_type x3, local copies, waits for them, and re-layouts, merge_patches(): grouped.astype(jnp.float32)  6.29 us
    dot_general x2, matrix products, merge_patches(): jnp.dot(merged, w_merge, preferred_element_type=jnp.float32)  5.98 us
    unnamed x47, local copies, waits for them, and re-layouts  5.96 us
    sub x1, matrix products, attend(): exp_scores = jnp.exp(scores - row_top)  5.93 us
  transfers between devices with their start and end apart: 8, of which 8 were waited for; matrix products, arithmetic and copies ran while one was open for 2% of the time, Pallas kernels for 0%

commit v1 on v0

v1 whole, which is shorter than its diff:
```python
import functools

import jax
import jax.numpy as jnp
from jax import lax
from jax.experimental import pallas as pl
from jax.experimental.pallas import tpu as pltpu
from jax.sharding import PartitionSpec as P

WLAT = 6
WLON = 12
PAIRS = 4
TOK = 144
FEAT = 512
EPS = 1e-05
BF = jnp.bfloat16
F32 = jnp.float32
MESH = pl.DeviceIdType.MESH


def dot(a, b):
    return jnp.dot(a, b, preferred_element_type=F32)


def dot_t(a, b):
    return lax.dot_general(a, b, (((1,), (1,)), ((), ())), preferred_element_type=F32)


def t_dot(a, b):
    return lax.dot_general(a, b, (((0,), (0,)), ((), ())), preferred_element_type=F32)


def kernel(
    behind_lat, behind_lon, halo_lat, halo_lon,
    shift_lat, shift_lon, gain_attn, gain_merge,
    inputs, w_qkv_hbm, w_out_hbm, w_merge_hbm, cot_coarse_hbm, cot_skip_hbm,
    coarse_hbm, skip_hbm, grad_hbm,
    own, ext, bext, gext, rext, gskip, skip, cot_skip, cot_coarse, coarse, out,
    w_qkv, w_out, w_merge,
    gm, merged, normed, norm, rstd, proj, mixed, soft, dproj, bias,
    local_sem, out_sem, send_sem, recv_sem,
):
    rows, cols = own.shape[0], own.shape[1]
    lat, lon = lax.axis_index("lat"), lax.axis_index("lon")
    nlat, nlon = lax.axis_size("lat"), lax.axis_size("lon")
    band = rows * nlat

    def device(step_lat, step_lon):
        return (lax.rem(lat + step_lat + nlat, nlat), lax.rem(lon + step_lon + nlon, nlon))

    dlat, dlon = (-1 if behind_lat else 1), (-1 if behind_lon else 1)
    steps = ((dlat, 0), (0, dlon), (dlat, dlon))
    own_r, own_c = (halo_lat if behind_lat else 0), (halo_lon if behind_lon else 0)
    halo_r, halo_c = (0 if behind_lat else rows), (0 if behind_lon else cols)
    back_r, back_c = (0 if behind_lat else halo_lat), (0 if behind_lon else halo_lon)
    bhalo_r, bhalo_c = (rows if behind_lat else 0), (cols if behind_lon else 0)
    edge_r, edge_c = (rows - halo_lat if behind_lat else 0), (cols - halo_lon if behind_lon else 0)
    bedge_r, bedge_c = (0 if behind_lat else rows - halo_lat), (0 if behind_lon else cols - halo_lon)

    def piece(ref, which, r, c, fr, fc):
        rr = pl.ds(fr, rows) if which == 1 else pl.ds(r, halo_lat)
        cc = pl.ds(fc, cols) if which == 0 else pl.ds(c, halo_lon)
        return ref.at[rr, cc]

    def ahead(phase, source, base_r, base_c, target):
        copies = []
        for which, (sr, sc) in enumerate(steps):
            copies.append(pltpu.make_async_remote_copy(
                src_ref=piece(source, which, base_r + edge_r, base_c + edge_c, base_r, base_c),
                dst_ref=piece(target, which, halo_r, halo_c, own_r, own_c),
                send_sem=send_sem.at[phase, which],
                recv_sem=recv_sem.at[phase, which],
                device_id=device(-sr, -sc),
                device_id_type=MESH,
            ))
        return copies

    def back(phase, ref):
        copies = []
        for which, (sr, sc) in enumerate(steps):
            copies.append(pltpu.make_async_remote_copy(
                src_ref=piece(ref, which, back_r + bedge_r, back_c + bedge_c, back_r, back_c),
                dst_ref=piece(ref, which, bhalo_r, bhalo_c, back_r, back_c),
                send_sem=send_sem.at[phase, which],
                recv_sem=recv_sem.at[phase, which],
                device_id=device(sr, sc),
                device_id_type=MESH,
            ))
        return copies

    loads = [
        pltpu.make_async_copy(src, dst, local_sem.at[i])
        for i, (src, dst) in enumerate((
            (cot_coarse_hbm, cot_coarse),
            (w_merge_hbm, w_merge),
            (inputs, own),
            (w_qkv_hbm, w_qkv),
            (w_out_hbm, w_out),
            (inputs, ext.at[pl.ds(own_r, rows), pl.ds(own_c, cols)]),
            (cot_skip_hbm, cot_skip),
        ))
    ]
    barrier = pltpu.get_barrier_semaphore()
    for sr, sc in steps:
        pl.semaphore_signal(barrier, inc=1, device_id=device(sr, sc), device_id_type=MESH)
        pl.semaphore_signal(barrier, inc=1, device_id=device(-sr, -sc), device_id_type=MESH)
    for load in loads:
        load.start()
    pl.semaphore_wait(barrier, 6)
    first = ahead(0, inputs, 0, 0, ext)
    for copy in first:
        copy.start()

    s_lat, s_lon = shift_lat[0], shift_lon[0]
    t_lat = s_lat - (WLAT - halo_lat) if behind_lat else s_lat
    t_lon = s_lon - (WLON - halo_lon) if behind_lon else s_lon
    li, lj = int(behind_lat), int(behind_lon)
    places = ((li, lj), (li, 1 - lj), (1 - li, lj), (1 - li, 1 - lj))

    def tile(slot):
        return pl.ds(slot * TOK, TOK)

    low = lax.broadcasted_iota(jnp.int32, (TOK, 128), 1) < 64
    zero = jnp.zeros((TOK, 128), BF)

    def both(x):
        return jnp.concatenate([jnp.where(low, x, zero), jnp.where(low, zero, x)], 0)

    def unite(x):
        return jnp.where(low, x[:TOK], x[TOK:])

    for wi in range(2):
        base = lax.rem(rows * lat - WLAT * li + WLAT * wi + band, band)
        edge = 2 * WLON * (band - s_lat - base)
        row_in = lax.broadcasted_iota(jnp.int32, (TOK, TOK), 0) >= edge
        col_in = lax.broadcasted_iota(jnp.int32, (TOK, TOK), 1) >= edge
        bias[wi] = jnp.where(row_in != col_in, F32(-1e30), F32(0.0))

    def norm_tokens(x, slot):
        mean = jnp.mean(x, -1, keepdims=True)
        centred = x - mean
        inv = lax.rsqrt(jnp.mean(centred * centred, -1, keepdims=True) + EPS)
        n = centred * inv
        norm[tile(slot)] = n
        rstd[tile(slot)] = jnp.broadcast_to(inv, (TOK, 128))
        normed[tile(slot)] = (n * gain_attn[...]).astype(BF)

    def attend(slot, p):
        at = pl.multiple_of(p * 128, 128)
        rr = tile(slot)
        q = both(proj[rr, pl.ds(at, 128)] * BF(0.125))
        k = proj[rr, pl.ds(FEAT + at, 128)]
        v = proj[rr, pl.ds(2 * FEAT + at, 128)]
        b = bias[places[slot][0]]
        scores = dot_t(q, k) + jnp.concatenate([b, b], 0)
        e = jnp.exp(scores - jnp.max(scores, -1, keepdims=True))
        w = (e * (1.0 / jnp.sum(e, -1, keepdims=True))).astype(BF)
        soft[slot, p] = w
        mixed[rr, pl.ds(at, 128)] = unite(dot(w, v)).astype(BF)

    def attend_back(slot, p):
        at = pl.multiple_of(p * 128, 128)
        rr = tile(slot)
        q = both(proj[rr, pl.ds(at, 128)] * BF(0.125))
        k = proj[rr, pl.ds(FEAT + at, 128)]
        v = proj[rr, pl.ds(2 * FEAT + at, 128)]
        g = both(mixed[rr, pl.ds(at, 128)])
        w = soft[slot, p]
        dw = dot_t(g, v)
        wf = w.astype(F32)
        ds = (wf * (dw - jnp.sum(dw * wf, -1, keepdims=True))).astype(BF)
        dproj[rr, pl.ds(at, 128)] = (unite(dot(ds, k)) * 0.125).astype(BF)
        dproj[rr, pl.ds(FEAT + at, 128)] = t_dot(ds, q).astype(BF)
        dproj[rr, pl.ds(2 * FEAT + at, 128)] = t_dot(w, g).astype(BF)

    def pairs(step, slots):
        if len(slots) == 1:
            for p in range(PAIRS):
                step(slots[0], p)
        else:
            def body(p, carry):
                for slot in slots:
                    step(slot, p)
                return carry
            lax.fori_loop(0, PAIRS, body, 0)

    def window(ref, slot):
        wi, wj = places[slot]
        x = ref[pl.ds(t_lat + WLAT * wi, WLAT), pl.ds(t_lon + WLON * wj, WLON)]
        return x.reshape(TOK, FEAT)

    def local_window(ref):
        return ref[pl.ds(s_lat, WLAT), pl.ds(s_lon, WLON)].reshape(TOK, FEAT)

    def put_window(ref, slot, x):
        wi, wj = places[slot]
        ref[pl.ds(back_r + WLAT * wi, WLAT), pl.ds(back_c + WLON * wj, WLON)] = x.reshape(
            WLAT, WLON, 2, FEAT
        )

    def run_forward(slots, fetch):
        lo, n = slots[0] * TOK, len(slots) * TOK
        for slot in slots:
            norm_tokens(fetch(slot).astype(F32), slot)
        proj[pl.ds(lo, n)] = dot(normed[pl.ds(lo, n)], w_qkv[...]).astype(BF)
        pairs(attend, slots)
        branch = dot(mixed[pl.ds(lo, n)], w_out[...]).astype(BF)
        for i, slot in enumerate(slots):
            put_window(bext, slot, branch[i * TOK:(i + 1) * TOK])

    def run_backward(slots, fetch):
        lo, n = slots[0] * TOK, len(slots) * TOK
        for slot in slots:
            normed[tile(slot)] = fetch(slot)
        mixed[pl.ds(lo, n)] = dot_t(normed[pl.ds(lo, n)], w_out[...]).astype(BF)
        pairs(attend_back, slots)
        dnormed = dot_t(dproj[pl.ds(lo, n)], w_qkv[...]).astype(BF)
        for i, slot in enumerate(slots):
            d = dnormed[i * TOK:(i + 1) * TOK].astype(F32) * gain_attn[...]
            nn = norm[tile(slot)]
            inv = rstd[tile(slot)][:, :1]
            dx = inv * (
                d - jnp.mean(d, -1, keepdims=True) - nn * jnp.mean(d * nn, -1, keepdims=True)
            )
            put_window(rext, slot, dx.astype(BF))

    loads[0].wait()
    loads[1].wait()
    gm[...] = dot_t(cot_coarse.reshape(TOK, 2 * FEAT)[...], w_merge[...]).astype(BF)
    loads[2].wait()
    loads[3].wait()
    loads[4].wait()
    run_forward((0,), lambda slot: local_window(own))
    loads[5].wait()
    for copy in first:
        copy.wait_recv()
    run_forward((1, 2, 3), lambda slot: window(ext, slot))
    second = back(1, bext)
    for copy in second:
        copy.start()
    loads[6].wait()
    for copy in second:
        copy.wait_recv()

    start_r, start_c = halo_lat - t_lat, halo_lon - t_lon
    skip[...] = (
        own[...].astype(F32)
        + bext[pl.ds(start_r, rows), pl.ds(start_c, cols)].astype(F32)
    ).astype(BF)
    skip_out = pltpu.make_async_copy(skip, skip_hbm, out_sem.at[0])
    skip_out.start()

    patches = (rows // 2, 2, cols // 2, 2, 2, FEAT)
    quarters = [(a, b) for a in range(2) for b in range(2)]

    def quarter(ref, a, b):
        return ref.reshape(*patches)[:, a, :, b].reshape(TOK, FEAT)

    parts = [quarter(skip, a, b).astype(F32) for a, b in quarters]
    width = 4 * FEAT
    mean = sum(jnp.sum(x, -1, keepdims=True) for x in parts) / width
    parts = [x - mean for x in parts]
    inv = lax.rsqrt(sum(jnp.sum(x * x, -1, keepdims=True) for x in parts) / width + EPS)
    parts = [x * inv for x in parts]
    grads = []
    for i, x in enumerate(parts):
        gain = gain_merge[:, pl.ds(i * FEAT, FEAT)]
        merged[:, pl.ds(i * FEAT, FEAT)] = (x * gain).astype(BF)
        grads.append(gm[:, pl.ds(i * FEAT, FEAT)].astype(F32) * gain)
    mean_g = sum(jnp.sum(g, -1, keepdims=True) for g in grads) / width
    mean_gx = sum(jnp.sum(g * x, -1, keepdims=True) for g, x in zip(grads, parts)) / width
    for (a, b), g, x in zip(quarters, grads, parts):
        d = (inv * (g - mean_g - x * mean_gx)).astype(BF) + quarter(cot_skip, a, b)
        gskip.reshape(*patches)[:, a, :, b] = d.reshape(rows // 2, cols // 2, 2, FEAT)
    gext[pl.ds(own_r, rows), pl.ds(own_c, cols)] = gskip[...]
    third = ahead(2, gext, own_r, own_c, gext)
    for copy in third:
        copy.start()

    coarse.reshape(TOK, 2 * FEAT)[...] = dot(merged[...], w_merge[...]).astype(BF)
    coarse_out = pltpu.make_async_copy(coarse, coarse_hbm, out_sem.at[1])
    coarse_out.start()
    run_backward((0,), lambda slot: local_window(gskip))
    for copy in third:
        copy.wait_recv()
    run_backward((1, 2, 3), lambda slot: window(gext, slot))
    fourth = back(3, rext)
    for copy in fourth:
        copy.start()
    for copy in fourth:
        copy.wait_recv()
    out[...] = gskip[...] + rext[pl.ds(start_r, rows), pl.ds(start_c, cols)]
    grad_out = pltpu.make_async_copy(out, grad_hbm, out_sem.at[2])
    grad_out.start()
    for copy in first + second + third + fourth:
        copy.wait_send()
    skip_out.wait()
    coarse_out.wait()
    grad_out.wait()


def block(behind_lat, behind_lon, halo_lat, halo_lon, ident, args):
    (inputs, shift_lat, shift_lon, gain_attn, w_qkv, w_out, gain_merge, w_merge,
     cot_coarse, cot_skip) = args
    rows, cols, lev, feat = inputs.shape
    wide = (rows + halo_lat, cols + halo_lon, lev, feat)
    tokens = rows * cols * lev
    smem = pl.BlockSpec(memory_space=pltpu.SMEM)
    vmem = pl.BlockSpec(memory_space=pltpu.VMEM)
    anyw = pl.BlockSpec(memory_space=pl.ANY)
    return pl.pallas_call(
        functools.partial(kernel, behind_lat, behind_lon, halo_lat, halo_lon),
        out_shape=(
            jax.ShapeDtypeStruct(cot_coarse.shape, BF),
            jax.ShapeDtypeStruct(inputs.shape, BF),
            jax.ShapeDtypeStruct(inputs.shape, BF),
        ),
        in_specs=[smem, smem, vmem, vmem] + [anyw] * 6,
        out_specs=(anyw, anyw, anyw),
        scratch_shapes=[
            pltpu.VMEM(inputs.shape, BF),
            pltpu.VMEM(wide, BF),
            pltpu.VMEM(wide, BF),
            pltpu.VMEM(wide, BF),
            pltpu.VMEM(wide, BF),
            pltpu.VMEM(inputs.shape, BF),
            pltpu.VMEM(inputs.shape, BF),
            pltpu.VMEM(inputs.shape, BF),
            pltpu.VMEM(cot_coarse.shape, BF),
            pltpu.VMEM(cot_coarse.shape, BF),
            pltpu.VMEM(inputs.shape, BF),
            pltpu.VMEM(w_qkv.shape, BF),
            pltpu.VMEM(w_out.shape, BF),
            pltpu.VMEM(w_merge.shape, BF),
            pltpu.VMEM((TOK, 4 * FEAT), BF),
            pltpu.VMEM((TOK, 4 * FEAT), BF),
            pltpu.VMEM((tokens, FEAT), BF),
            pltpu.VMEM((tokens, FEAT), F32),
            pltpu.VMEM((tokens, 128), F32),
            pltpu.VMEM((tokens, 3 * FEAT), BF),
            pltpu.VMEM((tokens, FEAT), BF),
            pltpu.VMEM((4, PAIRS, 2 * TOK, TOK), BF),
            pltpu.VMEM((tokens, 3 * FEAT), BF),
            pltpu.VMEM((2, TOK, TOK), F32),
            pltpu.SemaphoreType.DMA((7,)),
            pltpu.SemaphoreType.DMA((3,)),
            pltpu.SemaphoreType.DMA((4, 3)),
            pltpu.SemaphoreType.DMA((4, 3)),
        ],
        compiler_params=pltpu.CompilerParams(
            collective_id=ident, has_side_effects=True, vmem_limit_bytes=48 * 2**20
        ),
    )(
        shift_lat, shift_lon, gain_attn.reshape(1, -1), gain_merge.reshape(1, -1),
        inputs, w_qkv, w_out, w_merge, cot_coarse, cot_skip,
    )


def local(*args):
    return block(False, False, WLAT - 1, WLON - 1, 0, args)


def solution(mesh):
    tile = P("lat", "lon", None, None)
    return jax.shard_map(
        local,
        mesh=mesh,
        in_specs=(tile, P(), P(), P(), P(), P(), P(), P(), tile, tile),
        out_specs=(tile, tile, tile),
        check_vma=False,
    )
```

time: 213 us -> 90.4 us (0.42)
  the two profiles are of different devices: /device:TPU:0 before, /device:TPU:1 now
where the time goes in v1:
time: 90.4 us; the launch traced here: 90 us
  Pallas kernels  78.8 us (87%)
  local copies, waits for them, and re-layouts  9.25 us (10%)
  between operations  1.95 us (2%)
    pallas_call x1, Pallas kernels, block(): pl.pallas_call(functools.partial(kernel, behind_lat, behind_lon, halo_lat...  78.8 us
    unnamed x17, local copies, waits for them, and re-layouts  9.25 us

profile of v1, /device:TPU:1, one launch (start us, length us, event | category | flops | bytes accessed | tf_op | source)
XLA Modules:
  0.0 90.0 jit_solution(5171592439219663599)
XLA Ops:
  1.9 0.0 copy-start
  1.9 1.4 %copy-done = bf16[512,1536]{1,0:T(8,128)(2,1)S(1)} copy-done((bf16[512,1536]{1,0:T(8,128)(2,1)S(1)}, bf16[512,1536]{1,0:T(8,128)(2,1)}, u32[]{:S(2)}) %copy-start) | copy-done | bytes 1572888
  3.3 0.0 copy-start.1
  3.3 1.1 %copy-done.1 = bf16[12,24,2,512]{3,2,1,0:T(2,128)(2,1)S(1)} copy-done((bf16[12,24,2,512]{3,2,1,0:T(2,128)(2,1)S(1)}, bf16[12,24,2,512]{3,2,1,0:T(2,128)(2,1)}, u32[]{:S(2)}) %copy-start.1) | copy-done | bytes 589848
  4.4 0.0 copy-start.2
  4.4 1.1 %copy-done.2 = bf16[12,24,2,512]{3,2,1,0:T(2,128)(2,1)S(1)} copy-done((bf16[12,24,2,512]{3,2,1,0:T(2,128)(2,1)S(1)}, bf16[12,24,2,512]{3,2,1,0:T(2,128)(2,1)}, u32[]{:S(2)}) %copy-start.2) | copy-done | bytes 589848
  5.5 0.0 copy-start.3
  5.5 1.0 %copy-done.3 = bf16[512,512]{1,0:T(8,128)(2,1)S(1)} copy-done((bf16[512,512]{1,0:T(8,128)(2,1)S(1)}, bf16[512,512]{1,0:T(8,128)(2,1)}, u32[]{:S(2)}) %copy-start.3) | copy-done | bytes 524312
  6.5 0.0 copy-start.4
  6.5 1.0 %copy-done.4 = bf16[6,12,2,1024]{3,2,1,0:T(2,128)(2,1)S(1)} copy-done((bf16[6,12,2,1024]{3,2,1,0:T(2,128)(2,1)S(1)}, bf16[6,12,2,1024]{3,2,1,0:T(2,128)(2,1)}, u32[]{:S(2)}) %copy-start.4) | copy-done | bytes 294936
  7.5 0.0 copy-start.5
  7.5 0.7 copy-done.5
  8.2 0.0 copy-start.6
  8.2 0.7 copy-done.6
  8.8 78.8 %shard_map.121 = (bf16[6,12,2,1024]{3,2,1,0:T(2,128)(2,1)S(1)}, bf16[12,24,2,512]{3,2,1,0:T(2,128)(2,1)S(1)}, bf16[12,24,2,512]{3,2,1,0:T(2,128)(2,1)S(1)}) custom-call(s32[1]{0:T(128)S(6)} %copy.16.shift_lat, s32[1]{0:T(128)S(6)} %copy.17.shift_lon, f32[1,512]{1,0:T(1,128)S(1)} %bitcast.3, f32[1,2048]{1,0:T(1,128)S(1)} %bitcast.2, ...), custom_call_target="tpu_custom_call" | custom-call | tf_op jit(solution)/shard_map/pallas_call | solution.py:311
  87.7 0.7 copy.18
  88.4 0.8 copy.19
  89.2 0.8 copy.20
Async XLA Ops:
  1.9 1.4 %copy-start = (bf16[512,1536]{1,0:T(8,128)(2,1)S(1)}, bf16[512,1536]{1,0:T(8,128)(2,1)}, u32[]{:S(2)}) copy-start(bf16[512,1536]{1,0:T(8,128)(2,1)} %w_qkv_hbm.1) | copy-start | bytes 4718596
  3.3 1.1 %copy-start.1 = (bf16[12,24,2,512]{3,2,1,0:T(2,128)(2,1)S(1)}, bf16[12,24,2,512]{3,2,1,0:T(2,128)(2,1)}, u32[]{:S(2)}) copy-start(bf16[12,24,2,512]{3,2,1,0:T(2,128)(2,1)} %inputs.1) | copy-start | bytes 1769476
  4.4 1.1 %copy-start.2 = (bf16[12,24,2,512]{3,2,1,0:T(2,128)(2,1)S(1)}, bf16[12,24,2,512]{3,2,1,0:T(2,128)(2,1)}, u32[]{:S(2)}) copy-start(bf16[12,24,2,512]{3,2,1,0:T(2,128)(2,1)} %cot_skip_hbm.1) | copy-start | bytes 1769476
  5.5 1.0 %copy-start.3 = (bf16[512,512]{1,0:T(8,128)(2,1)S(1)}, bf16[512,512]{1,0:T(8,128)(2,1)}, u32[]{:S(2)}) copy-start(bf16[512,512]{1,0:T(8,128)(2,1)} %w_out_hbm.1) | copy-start | bytes 1572868
  6.5 1.0 %copy-start.4 = (bf16[6,12,2,1024]{3,2,1,0:T(2,128)(2,1)S(1)}, bf16[6,12,2,1024]{3,2,1,0:T(2,128)(2,1)}, u32[]{:S(2)}) copy-start(bf16[6,12,2,1024]{3,2,1,0:T(2,128)(2,1)} %cot_coarse_hbm.1) | copy-start | bytes 884740
  7.5 0.7 copy-start.5
  8.2 0.7 copy-start.6

commit v2 on v1

v2 whole, which is shorter than its diff:
```python
import jax
import jax.numpy as jnp
from jax import lax
from jax.experimental import pallas as pl
from jax.experimental.pallas import tpu as pltpu
from jax.sharding import PartitionSpec as P

WLAT = 6
WLON = 12
PAIRS = 4
TOK = 144
FEAT = 512
EPS = 1e-05
BF = jnp.bfloat16
F32 = jnp.float32
MESH = pl.DeviceIdType.MESH
VMEM = 62 * 2**20
HLAT = WLAT // 2
HLON = WLON // 2
AROUND = ((0, 1), (0, -1), (1, 0), (-1, 0), (1, 1), (-1, -1), (1, -1), (-1, 1))


def dot(a, b):
    return jnp.dot(a, b, preferred_element_type=F32)


def dot_t(a, b):
    return lax.dot_general(a, b, (((1,), (1,)), ((), ())), preferred_element_type=F32)


def t_dot(a, b):
    return lax.dot_general(a, b, (((0,), (0,)), ((), ())), preferred_element_type=F32)


def kernel(
    shift_lat_hbm, shift_lon_hbm, gain_attn_hbm, gain_merge_hbm,
    inputs, w_qkv_hbm, w_out_hbm, w_merge_hbm, cot_coarse_hbm, cot_skip_hbm,
    coarse_hbm, skip_hbm, grad_hbm,
    shift_lat, shift_lon, gain_attn, gain_merge,
    own, ext, bext, gext, rext, wins, gskip, skip, cot_skip, cot_coarse, coarse, out,
    w_qkv, w_out, w_merge,
    gm, merged, normed, norm, rstd, proj, mixed, soft, dproj, bias,
    local_sem, out_sem, send_sem, recv_sem,
):
    rows, cols = own.shape[0], own.shape[1]
    lat, lon = lax.axis_index("lat"), lax.axis_index("lon")
    nlat, nlon = lax.axis_size("lat"), lax.axis_size("lon")
    band = rows * nlat

    def device(step_lat, step_lon):
        return (lax.rem(lat + step_lat + nlat, nlat), lax.rem(lon + step_lon + nlon, nlon))

    def span(step, size, halo, base):
        if step == 0:
            return pl.ds(base, size), pl.ds(halo, size)
        if step > 0:
            return pl.ds(base + size - halo, halo), pl.ds(0, halo)
        return pl.ds(base, halo), pl.ds(halo + size, halo)

    def exchange(phase, source, base_r, base_c, target):
        copies = []
        for i, (dr, dc) in enumerate(AROUND):
            sr, tr = span(dr, rows, HLAT, base_r)
            sc, tc = span(dc, cols, HLON, base_c)
            copies.append(pltpu.make_async_remote_copy(
                src_ref=source.at[sr, sc],
                dst_ref=target.at[tr, tc],
                send_sem=send_sem.at[phase, i],
                recv_sem=recv_sem.at[phase, i],
                device_id=device(dr, dc),
                device_id_type=MESH,
            ))
        return copies

    inner = (pl.ds(HLAT, rows), pl.ds(HLON, cols))
    loads = [
        pltpu.make_async_copy(src, dst, local_sem.at[i])
        for i, (src, dst) in enumerate((
            (shift_lat_hbm, shift_lat),
            (shift_lon_hbm, shift_lon),
            (cot_coarse_hbm, cot_coarse),
            (w_merge_hbm, w_merge),
            (gain_attn_hbm, gain_attn),
            (inputs, own),
            (w_qkv_hbm, w_qkv),
            (w_out_hbm, w_out),
            (inputs, ext.at[inner]),
            (cot_skip_hbm, cot_skip),
            (gain_merge_hbm, gain_merge),
        ))
    ]
    barrier = pltpu.get_barrier_semaphore()
    for dr, dc in AROUND:
        pl.semaphore_signal(barrier, inc=1, device_id=device(dr, dc), device_id_type=MESH)
    for load in loads:
        load.start()
    pl.semaphore_wait(barrier, len(AROUND))
    first = exchange(0, inputs, 0, 0, ext)
    for copy in first:
        copy.start()

    loads[0].wait()
    loads[1].wait()
    s_lat, s_lon = shift_lat[0], shift_lon[0]
    back_lat = (s_lat > HLAT).astype(jnp.int32)
    back_lon = (s_lon > HLON).astype(jnp.int32)
    ahead_r = HLAT + s_lat - WLAT * back_lat
    ahead_c = HLON + s_lon - WLON * back_lon
    home_r = HLAT - s_lat + WLAT * back_lat
    home_c = HLON - s_lon + WLON * back_lon
    places = tuple(
        (jnp.abs(a - back_lat), jnp.abs(b - back_lon)) for a in range(2) for b in range(2)
    )

    def tile(slot):
        return pl.ds(slot * TOK, TOK)

    low = lax.broadcasted_iota(jnp.int32, (TOK, 128), 1) < 64
    zero = jnp.zeros((TOK, 128), BF)

    def both(x):
        return jnp.concatenate([jnp.where(low, x, zero), jnp.where(low, zero, x)], 0)

    def unite(x):
        return jnp.where(low, x[:TOK], x[TOK:])

    start = rows * lat + WLAT * (1 - 2 * back_lat)
    start = jnp.where(start < 0, start + band, start)
    edge = 2 * WLON * (band - s_lat - start)
    row_in = lax.broadcasted_iota(jnp.int32, (TOK, TOK), 0) >= edge
    col_in = lax.broadcasted_iota(jnp.int32, (TOK, TOK), 1) >= edge
    apart = jnp.where(row_in != col_in, F32(-1e30), F32(0.0))
    bias[...] = jnp.concatenate([apart, apart], 1)

    def norm_tokens(x, slot):
        mean = jnp.mean(x, -1, keepdims=True)
        centred = x - mean
        inv = lax.rsqrt(jnp.mean(centred * centred, -1, keepdims=True) + EPS)
        n = centred * inv
        norm[tile(slot)] = n
        rstd[tile(slot)] = jnp.broadcast_to(inv, (TOK, 128))
        normed[tile(slot)] = (n * gain_attn[...]).astype(BF)

    def attend(slot, p):
        at = p * 128
        rr = tile(slot)
        q = both(proj[rr, pl.ds(at, 128)] * BF(0.125))
        k = proj[rr, pl.ds(FEAT + at, 128)]
        v = proj[rr, pl.ds(2 * FEAT + at, 128)]
        scores = dot_t(k, q)
        if slot >= 2:
            scores = scores + bias[...]
        e = jnp.exp(scores - jnp.max(scores, 0, keepdims=True))
        w = (e * (1.0 / jnp.sum(e, 0, keepdims=True))).astype(BF)
        soft[slot, p] = w
        mixed[rr, pl.ds(at, 128)] = unite(t_dot(w, v)).astype(BF)

    def attend_back(slot, p):
        at = p * 128
        rr = tile(slot)
        q = both(proj[rr, pl.ds(at, 128)] * BF(0.125))
        k = proj[rr, pl.ds(FEAT + at, 128)]
        v = proj[rr, pl.ds(2 * FEAT + at, 128)]
        g = both(mixed[rr, pl.ds(at, 128)])
        w = soft[slot, p]
        dw = dot_t(v, g)
        wf = w.astype(F32)
        ds = (wf * (dw - jnp.sum(dw * wf, 0, keepdims=True))).astype(BF)
        dproj[rr, pl.ds(at, 128)] = (unite(t_dot(ds, k)) * 0.125).astype(BF)
        dproj[rr, pl.ds(FEAT + at, 128)] = dot(ds, q).astype(BF)
        dproj[rr, pl.ds(2 * FEAT + at, 128)] = dot(w, g).astype(BF)

    def pairs(step, slots):
        for slot in slots:
            for p in range(PAIRS):
                step(slot, p)

    def window(ref, slot):
        wi, wj = places[slot]
        x = ref[pl.ds(ahead_r + WLAT * wi, WLAT), pl.ds(ahead_c + WLON * wj, WLON)]
        return x.reshape(TOK, FEAT)

    def local_window(ref):
        return ref[pl.ds(s_lat, WLAT), pl.ds(s_lon, WLON)].reshape(TOK, FEAT)

    def place(ref):
        for a in range(2):
            for b in range(2):
                slot = 2 * jnp.abs(a - back_lat) + jnp.abs(b - back_lon)
                ref[pl.ds(HLAT + WLAT * a, WLAT), pl.ds(HLON + WLON * b, WLON)] = wins[slot]

    def run_forward(slots, fetch):
        lo, n = slots[0] * TOK, len(slots) * TOK
        for slot in slots:
            norm_tokens(fetch(slot).astype(F32), slot)
        proj[pl.ds(lo, n)] = dot(normed[pl.ds(lo, n)], w_qkv[...]).astype(BF)
        pairs(attend, slots)
        branch = dot(mixed[pl.ds(lo, n)], w_out[...]).astype(BF)
        for i, slot in enumerate(slots):
            wins[slot] = branch[i * TOK:(i + 1) * TOK].reshape(WLAT, WLON, 2, FEAT)

    def run_backward(slots, fetch):
        lo, n = slots[0] * TOK, len(slots) * TOK
        for slot in slots:
            normed[tile(slot)] = fetch(slot)
        mixed[pl.ds(lo, n)] = dot_t(normed[pl.ds(lo, n)], w_out[...]).astype(BF)
        pairs(attend_back, slots)
        dnormed = dot_t(dproj[pl.ds(lo, n)], w_qkv[...]).astype(BF)
        for i, slot in enumerate(slots):
            d = dnormed[i * TOK:(i + 1) * TOK].astype(F32) * gain_attn[...]
            nn = norm[tile(slot)]
            inv = rstd[tile(slot)][:, :1]
            dx = inv * (
                d - jnp.mean(d, -1, keepdims=True) - nn * jnp.mean(d * nn, -1, keepdims=True)
            )
            wins[slot] = dx.astype(BF).reshape(WLAT, WLON, 2, FEAT)

    loads[2].wait()
    loads[3].wait()
    gm[...] = dot_t(cot_coarse.reshape(TOK, 2 * FEAT)[...], w_merge[...]).astype(BF)
    for load in loads[4:8]:
        load.wait()
    run_forward((0,), lambda slot: local_window(own))
    loads[8].wait()
    for copy in first:
        copy.wait_recv()
    run_forward((1, 2, 3), lambda slot: window(ext, slot))
    place(bext)
    second = exchange(1, bext, HLAT, HLON, bext)
    for copy in second:
        copy.start()
    loads[9].wait()
    loads[10].wait()
    for copy in second:
        copy.wait_recv()

    skip[...] = (
        own[...].astype(F32) + bext[pl.ds(home_r, rows), pl.ds(home_c, cols)].astype(F32)
    ).astype(BF)
    skip_out = pltpu.make_async_copy(skip, skip_hbm, out_sem.at[0])
    skip_out.start()

    patches = (rows // 2, 2, cols // 2, 2, 2, FEAT)
    quarters = [(a, b) for a in range(2) for b in range(2)]

    def quarter(ref, a, b):
        return ref.reshape(*patches)[:, a, :, b].reshape(TOK, FEAT)

    parts = [quarter(skip, a, b).astype(F32) for a, b in quarters]
    width = 4 * FEAT
    mean = sum(jnp.sum(x, -1, keepdims=True) for x in parts) / width
    parts = [x - mean for x in parts]
    inv = lax.rsqrt(sum(jnp.sum(x * x, -1, keepdims=True) for x in parts) / width + EPS)
    parts = [x * inv for x in parts]
    grads = []
    for i, x in enumerate(parts):
        gain = gain_merge[:, pl.ds(i * FEAT, FEAT)]
        merged[:, pl.ds(i * FEAT, FEAT)] = (x * gain).astype(BF)
        grads.append(gm[:, pl.ds(i * FEAT, FEAT)].astype(F32) * gain)
    mean_g = sum(jnp.sum(g, -1, keepdims=True) for g in grads) / width
    mean_gx = sum(jnp.sum(g * x, -1, keepdims=True) for g, x in zip(grads, parts)) / width
    for (a, b), g, x in zip(quarters, grads, parts):
        d = (inv * (g - mean_g - x * mean_gx)).astype(BF) + quarter(cot_skip, a, b)
        gskip.reshape(*patches)[:, a, :, b] = d.reshape(rows // 2, cols // 2, 2, FEAT)
    gext[inner] = gskip[...]
    third = exchange(2, gext, HLAT, HLON, gext)
    for copy in third:
        copy.start()

    coarse.reshape(TOK, 2 * FEAT)[...] = dot(merged[...], w_merge[...]).astype(BF)
    coarse_out = pltpu.make_async_copy(coarse, coarse_hbm, out_sem.at[1])
    coarse_out.start()
    run_backward((0,), lambda slot: local_window(gskip))
    for copy in third:
        copy.wait_recv()
    run_backward((1, 2, 3), lambda slot: window(gext, slot))
    place(rext)
    fourth = exchange(3, rext, HLAT, HLON, rext)
    for copy in fourth:
        copy.start()
    for copy in fourth:
        copy.wait_recv()
    out[...] = gskip[...] + rext[pl.ds(home_r, rows), pl.ds(home_c, cols)]
    grad_out = pltpu.make_async_copy(out, grad_hbm, out_sem.at[2])
    grad_out.start()
    for copy in first + second + third + fourth:
        copy.wait_send()
    skip_out.wait()
    coarse_out.wait()
    grad_out.wait()


def local(
    inputs, shift_lat, shift_lon, gain_attn, w_qkv, w_out, gain_merge, w_merge, cot_coarse, cot_skip
):
    rows, cols, lev, feat = inputs.shape
    wide = (rows + 2 * HLAT, cols + 2 * HLON, lev, feat)
    tokens = rows * cols * lev
    hbm = pl.BlockSpec(memory_space=pltpu.HBM)
    anyw = pl.BlockSpec(memory_space=pl.ANY)
    return pl.pallas_call(
        kernel,
        out_shape=(
            jax.ShapeDtypeStruct(cot_coarse.shape, BF),
            jax.ShapeDtypeStruct(inputs.shape, BF),
            jax.ShapeDtypeStruct(inputs.shape, BF),
        ),
        in_specs=[hbm] * 10,
        out_specs=(anyw, anyw, anyw),
        scratch_shapes=[
            pltpu.SMEM((1,), jnp.int32),
            pltpu.SMEM((1,), jnp.int32),
            pltpu.VMEM((1, feat), F32),
            pltpu.VMEM((1, 4 * feat), F32),
            pltpu.VMEM(inputs.shape, BF),
            pltpu.VMEM(wide, BF),
            pltpu.VMEM(wide, BF),
            pltpu.VMEM(wide, BF),
            pltpu.VMEM(wide, BF),
            pltpu.VMEM((4, WLAT, WLON, lev, feat), BF),
            pltpu.VMEM(inputs.shape, BF),
            pltpu.VMEM(inputs.shape, BF),
            pltpu.VMEM(inputs.shape, BF),
            pltpu.VMEM(cot_coarse.shape, BF),
            pltpu.VMEM(cot_coarse.shape, BF),
            pltpu.VMEM(inputs.shape, BF),
            pltpu.VMEM(w_qkv.shape, BF),
            pltpu.VMEM(w_out.shape, BF),
            pltpu.VMEM(w_merge.shape, BF),
            pltpu.VMEM((TOK, 4 * FEAT), BF),
            pltpu.VMEM((TOK, 4 * FEAT), BF),
            pltpu.VMEM((tokens, FEAT), BF),
            pltpu.VMEM((tokens, FEAT), F32),
            pltpu.VMEM((tokens, 128), F32),
            pltpu.VMEM((tokens, 3 * FEAT), BF),
            pltpu.VMEM((tokens, FEAT), BF),
            pltpu.VMEM((4, PAIRS, TOK, 2 * TOK), BF),
            pltpu.VMEM((tokens, 3 * FEAT), BF),
            pltpu.VMEM((TOK, 2 * TOK), F32),
            pltpu.SemaphoreType.DMA((11,)),
            pltpu.SemaphoreType.DMA((3,)),
            pltpu.SemaphoreType.DMA((4, len(AROUND))),
            pltpu.SemaphoreType.DMA((4, len(AROUND))),
        ],
        compiler_params=pltpu.CompilerParams(
            collective_id=0, has_side_effects=True, vmem_limit_bytes=VMEM
        ),
    )(
        shift_lat, shift_lon, gain_attn.reshape(1, -1), gain_merge.reshape(1, -1),
        inputs, w_qkv, w_out, w_merge, cot_coarse, cot_skip,
    )


def solution(mesh):
    tile = P("lat", "lon", None, None)
    return jax.shard_map(
        local,
        mesh=mesh,
        in_specs=(tile, P(), P(), P(), P(), P(), P(), P(), tile, tile),
        out_specs=(tile, tile, tile),
        check_vma=False,
    )
```

time: 90.4 us -> 71.3 us (0.79)
  Pallas kernels: 78.8 us -> 62.5 us
  local copies, waits for them, and re-layouts: 9.25 us -> 6.62 us
    pallas_call x1, Pallas kernels: 78.8 us -> 62.5 us  [local(): pl.pallas_call(kernel, out_shape=(jax.ShapeDtypeStruct(cot_coarse.shape,...]
    unnamed x17 -> x3, local copies, waits for them, and re-layouts: 9.25 us -> 6.62 us
where the time goes in v2:
time: 71.3 us; the launch traced here: 71.1 us
  Pallas kernels  62.5 us (88%)
  local copies, waits for them, and re-layouts  6.62 us (9%)
  between operations  1.93 us (3%)
    pallas_call x1, Pallas kernels, local(): pl.pallas_call(kernel, out_shape=(jax.ShapeDtypeStruct(cot_coarse.shape,...  62.5 us
    unnamed x3, local copies, waits for them, and re-layouts  6.62 us

profile of v2, /device:TPU:1, one launch (start us, length us, event | category | flops | bytes accessed | tf_op | source)
XLA Modules:
  0.0 71.1 jit_solution(15937100389655370635)
XLA Ops:
  1.9 62.5 %shard_map.121 = (bf16[6,12,2,1024]{3,2,1,0:T(2,128)(2,1)}, bf16[12,24,2,512]{3,2,1,0:T(2,128)(2,1)}, bf16[12,24,2,512]{3,2,1,0:T(2,128)(2,1)}) custom-call(s32[1]{0:T(128)S(6)} %copy.16.shift_lat_hbm, s32[1]{0:T(128)S(6)} %copy.17.shift_lon_hbm, f32[1,512]{1,0:T(1,128)} %bitcast.3, f32[1,2048]{1,0:T(1,128)} %bitcast.2, bf16[12,24,2,512]{3,2,1,0:T(2,128)(2,1)} %inputs.1, ...), custom_call_target="tpu_custom_call" | custom-call | tf_op jit(solution)/shard_map/pallas_call | solution.py:301
  64.5 1.9 %copy.18 = bf16[6,12,2,1024]{3,2,1,0:T(2,128)(2,1)} copy(bf16[6,12,2,1024]{3,2,1,0:T(2,128)(2,1)} %get-tuple-element.6) | data formatting | bytes 589824
  66.3 2.4 %copy.19 = bf16[12,24,2,512]{3,2,1,0:T(2,128)(2,1)} copy(bf16[12,24,2,512]{3,2,1,0:T(2,128)(2,1)} %get-tuple-element.7) | data formatting | bytes 1179648
  68.7 2.4 %copy.20 = bf16[12,24,2,512]{3,2,1,0:T(2,128)(2,1)} copy(bf16[12,24,2,512]{3,2,1,0:T(2,128)(2,1)} %get-tuple-element.8) | data formatting | bytes 1179648
